TPU v7x, 256 devices: a whole 4x4x8 slice. The times are simulated.
256 devices in a mesh: ctx: 32 (over y, x, z_lo), head: 8 (over z_hi, core).
Axes of the slice: x: 4, y: 4, z: 8 (z_hi: 4, z_lo: 2; z = z_hi * 2 + z_lo), core: 2. Of those that a mesh axis runs over, the one named last changes fastest.
Arguments:
- light_query: bfloat16 [16384, 4096], P('ctx', 'head'), may hold values from -6 to 6
- light_key: bfloat16 [16384, 4096], P('ctx', 'head'), may hold values from -6 to 6
- light_value: bfloat16 [16384, 4096], P('ctx', 'head'), may hold values from -6 to 6
- light_gate: bfloat16 [16384, 4096], P('ctx', 'head'), may hold values from -6 to 6
- norm_gain: float32 [4096], P('head'), may hold values from 0.1 to 1.9
- decay_exponent: int32 [32], P('head'), may hold values from 1 to 2048, as said below
- soft_query: bfloat16 [16384, 4096], P('ctx', 'head'), may hold values from -45 to 45
- soft_key: bfloat16 [16384, 4096], P('ctx', 'head'), may hold values from -6 to 6
- soft_value: bfloat16 [16384, 4096], P('ctx', 'head'), may hold values from -6 to 6
Outputs:
- light_output: bfloat16 [16384, 4096], P('ctx', 'head')
- soft_output: bfloat16 [16384, 4096], P('ctx', 'head')
Inputs may be any that keep to these rules, and one draw needn't show every extreme that they name: Each head decays by exp(-decay_exponent / 65536) a token; the exponents are powers of two.
All inputs are finite; a program needn't handle non-finite values.
Results may differ from a plain program's by a relative error of at most 0.0096.
Values may be sent and summed in bfloat16 or wider, within the bound.
A program may use at most 128 MiB of HBM per device.

v0:
```python
import jax
import jax.numpy as jnp
from jax import lax
from jax.sharding import PartitionSpec as P

HEADS = 32
HD = 128


def body(
    light_query,
    light_key,
    light_value,
    light_gate,
    norm_gain,
    decay_exponent,
    soft_query,
    soft_key,
    soft_value,
):
    tokens = light_query.shape[0]
    local_heads = light_query.shape[1] // HD
    device = lax.axis_index("ctx")
    log_decay = -decay_exponent.astype(jnp.float32) / 65536.0
    queries = light_query.reshape(tokens, local_heads, HD)
    keys_local = light_key.reshape(tokens, local_heads, HD)
    values_local = light_value.reshape(tokens, local_heads, HD)
    positions = jnp.arange(tokens, dtype=jnp.float32)
    offsets = positions[:, None] - positions[None, :]
    decay_mask = jnp.where(
        offsets[None] >= 0, jnp.exp(jnp.maximum(offsets, 0.0)[None] * log_decay[:, None, None]), 0.0
    )
    scores = jnp.einsum("thd,shd->hts", queries, keys_local, preferred_element_type=jnp.float32)
    weighted = (scores * decay_mask).astype(jnp.bfloat16)
    intra = jnp.einsum("hts,she->the", weighted, values_local, preferred_element_type=jnp.float32)
    key_decay = jnp.exp((tokens - 1.0 - positions)[:, None] * log_decay[None, :])
    decayed_keys = keys_local.astype(jnp.float32) * key_decay[:, :, None]
    local_state = jnp.einsum(
        "shd,she->hde",
        decayed_keys,
        values_local.astype(jnp.float32),
        precision=lax.Precision.HIGHEST,
    )
    pieces = lax.all_gather(
        local_state[None].astype(jnp.bfloat16), "ctx", axis=0, tiled=True
    ).astype(jnp.float32)
    count = pieces.shape[0]
    sources = jnp.arange(count, dtype=jnp.int32)
    distance = (device - 1 - sources).astype(jnp.float32)
    factors = jnp.where(
        distance[:, None] >= 0,
        jnp.exp(jnp.maximum(distance, 0.0)[:, None] * tokens * log_decay[None, :]),
        0.0,
    )
    incoming = jnp.zeros_like(local_state) + jnp.einsum(
        "nh,nhde->hde", factors, pieces, precision=lax.Precision.HIGHEST
    )
    inter = jnp.einsum(
        "thd,hde->the", queries.astype(jnp.float32), incoming, precision=lax.Precision.HIGHEST
    )
    row_decay = jnp.exp((positions + 1.0)[:, None] * log_decay[None, :])
    mixed = (intra + row_decay[:, :, None] * inter).reshape(tokens, local_heads * HD)
    square_sum = lax.psum(jnp.sum(mixed * mixed, axis=1), "head")
    row_scale = lax.rsqrt(square_sum / (HEADS * HD) + 1e-05)
    light_output = (
        mixed
        * row_scale[:, None]
        * norm_gain[None, :]
        * jax.nn.sigmoid(light_gate.astype(jnp.float32))
    ).astype(jnp.bfloat16)
    scale = HD ** (-0.5)
    soft_queries = soft_query.reshape(tokens, local_heads, HD)
    query_positions = device * tokens + jnp.arange(tokens, dtype=jnp.int32)
    last_query = device * tokens + tokens - 1
    start_max = jnp.full((local_heads, tokens), -1e30, jnp.float32)
    start_total = jnp.zeros((local_heads, tokens), jnp.float32)
    start_accum = jnp.zeros((local_heads, tokens, HD), jnp.float32)
    key_piece = lax.all_gather(soft_key, "ctx", axis=0, tiled=True)
    value_piece = lax.all_gather(soft_value, "ctx", axis=0, tiled=True)
    count = key_piece.shape[0]
    width = 512
    key_parts = key_piece.reshape(count // width, width, local_heads, HD)
    value_parts = value_piece.reshape(count // width, width, local_heads, HD)
    part_starts = width * jnp.arange(count // width, dtype=jnp.int32)

    def one_part(state, inputs):
        key_part, value_part, part_start = inputs

        def compute(current):
            row_max, total, accum = current
            key_positions = part_start + jnp.arange(width, dtype=jnp.int32)
            causal = (query_positions[:, None] >= key_positions[None, :])[None]
            part_scores = (
                jnp.einsum(
                    "thd,shd->hts", soft_queries, key_part, preferred_element_type=jnp.float32
                )
                * scale
            )
            part_scores = jnp.where(causal, part_scores, -1e30)
            new_max = jnp.maximum(row_max, jnp.max(part_scores, axis=2))
            expo = jnp.where(causal, jnp.exp(part_scores - new_max[:, :, None]), 0.0)
            shrink = jnp.exp(row_max - new_max)
            new_total = total * shrink + jnp.sum(expo, axis=2)
            probs = expo.astype(jnp.bfloat16)
            product = jnp.einsum(
                "hts,she->hte", probs, value_part, preferred_element_type=jnp.float32
            )
            return (new_max, new_total, accum * shrink[:, :, None] + product)

        def keep(current):
            return current

        return (lax.cond(part_start <= last_query, compute, keep, state), None)

    result, unused_parts = lax.scan(
        one_part, (start_max, start_total, start_accum), (key_parts, value_parts, part_starts)
    )
    final_max, final_total, final_accum = result
    attended = (final_accum / final_total[:, :, None]).astype(jnp.bfloat16)
    soft_output = attended.transpose(1, 0, 2).reshape(tokens, local_heads * HD)
    return (light_output, soft_output)


def solution(mesh):
    return jax.shard_map(
        body,
        mesh=mesh,
        in_specs=(
            P("ctx", "head"),
            P("ctx", "head"),
            P("ctx", "head"),
            P("ctx", "head"),
            P("head"),
            P("head"),
            P("ctx", "head"),
            P("ctx", "head"),
            P("ctx", "head"),
        ),
        out_specs=(P("ctx", "head"), P("ctx", "head")),
        check_vma=False,
    )
```

profile of v0, /device:TPU:28, one launch (start us, length us, event | category | flops | bytes accessed | tf_op | source)
XLA Modules:
  0.0 1195.5 jit_solution(14863553277986011177)
XLA Ops:
  15.3 3.7 fusion.22
  19.0 156.9 %all-gather.9.cloned.1.call-done = bf16[128,128,128]{2,1,0:T(8,128)(2,1)} async-done(((bf16[4,128,128]{2,1,0:T(8,128)(2,1)}), bf16[128,128,128]{2,1,0:T(8,128)(2,1)}) %all-gather.9.cloned.1.call-update) | async-done | bytes 4194320 | tf_op jit(solution)/shard_map/all_gather | solution.py:44
  175.9 3.2 multiply_reduce_fusion
  180.2 14.4 %psum.7 = f32[512]{0:T(512)S(1)} all-reduce(f32[512]{0:T(512)S(1)} %get-tuple-element.217), channel_id=1, replica_groups=mesh['ctx'=32,'head'=8] {'head'}, use_global_device_ids=true, to_apply=%region_1.2 | all-reduce | flops 512 | bytes 4096 | tf_op jit(solution)/shard_map/psum | solution.py:63
  196.7 350.7 %all-gather.5.cloned.1.call-done = bf16[16384,512]{1,0:T(8,128)(2,1)} async-done(((bf16[512,512]{1,0:T(8,128)(2,1)}), bf16[16384,512]{1,0:T(8,128)(2,1)}) %all-gather.5.cloned.1.call-update) | async-done | bytes 16777232 | tf_op jit(solution)/shard_map/all_gather | solution.py:78
  547.5 23.7 %reshape.173 = bf16[32,512,4,128]{3,2,1,0:T(4,128)(2,1)} reshape(bf16[16384,512]{1,0:T(8,128)(2,1)} %all-gather.5.cloned.1.call-done) | data formatting | bytes 33554432 | tf_op jit(solution)/shard_map/reshape | solution.py:82
  571.2 15.1 %copy.42 = bf16[32,512,4,128]{3,1,2,0:T(8,128)(2,1)} copy(bf16[32,512,4,128]{3,2,1,0:T(4,128)(2,1)} %reshape.173) | data formatting | bytes 33554432
  586.3 326.9 %all-gather.7.cloned.1.call-done = bf16[16384,512]{1,0:T(8,128)(2,1)} async-done(((bf16[512,512]{1,0:T(8,128)(2,1)}), bf16[16384,512]{1,0:T(8,128)(2,1)}) %all-gather.7.cloned.1.call-update) | async-done | bytes 16777232 | tf_op jit(solution)/shard_map/all_gather | solution.py:79
  913.2 23.7 %reshape.174 = bf16[32,512,4,128]{3,2,1,0:T(4,128)(2,1)} reshape(bf16[16384,512]{1,0:T(8,128)(2,1)} %all-gather.7.cloned.1.call-done) | data formatting | bytes 33554432 | tf_op jit(solution)/shard_map/reshape | solution.py:83
  936.9 15.1 %copy.44 = bf16[32,512,4,128]{3,1,2,0:T(8,128)(2,1)} copy(bf16[32,512,4,128]{3,2,1,0:T(4,128)(2,1)} %reshape.174) | data formatting | bytes 33554432
  952.1 235.7 %while.15 = (s32[]{:T(128)}, f32[4,512]{1,0:T(4,128)S(1)}, f32[4,512]{1,0:T(4,128)S(1)}, f32[4,512,128]{2,1,0:T(8,128)S(1)}, s32[32]{0:T(128)S(1)}, /*index=5*/s...) while((s32[]{:T(128)}, f32[4,512]{1,0:T(4,128)S(1)}, ...), condition=%wide.region_7.8_spmd.clone, body=%wide.region_2.7_spmd.clone.sunk | while | flops 551293952 | bytes 17446176 | solution.py:115
  953.3 6.7 conditional.3
  957.2 2.9 fusion.8
  961.3 6.7 conditional.3
  965.2 2.9 fusion.8
  969.3 6.7 conditional.3
  973.2 2.9 fusion.8
  977.3 6.7 conditional.3
  981.2 2.9 fusion.8
  985.3 6.7 conditional.3
  989.2 2.9 fusion.8
  993.3 6.7 conditional.3
  997.2 2.9 fusion.8
  1001.3 6.7 conditional.3
  1005.2 2.9 fusion.8
  1009.3 6.7 conditional.3
  1013.2 2.9 fusion.8
  1017.3 6.7 conditional.3
  1021.2 2.9 fusion.8
  1025.3 6.7 conditional.3
  1029.2 2.9 fusion.8
  1033.3 6.7 conditional.3
  1037.2 2.9 fusion.8
  1041.3 6.7 conditional.3
  1045.2 2.9 fusion.8
  1049.3 6.7 conditional.3
  1053.1 2.9 fusion.8
  1057.3 6.7 conditional.3
  1061.1 2.9 fusion.8
  1065.3 6.7 conditional.3
  1069.1 2.9 fusion.8
  1073.3 6.7 conditional.3
  1077.1 2.9 fusion.8
  1081.3 6.7 conditional.3
  1089.3 6.7 conditional.3
  1097.3 6.7 conditional.3
  1105.2 6.7 conditional.3
  1113.2 6.7 conditional.3
  1117.1 2.9 fusion.8
  1121.2 6.7 conditional.3
  1129.2 6.7 conditional.3
  1133.1 2.9 fusion.8
  1137.2 6.7 conditional.3
  1141.1 2.9 fusion.8
  1145.2 6.7 conditional.3
  1149.1 2.9 fusion.8
  1153.2 6.7 conditional.3
  1157.1 2.9 fusion.8
  1161.2 6.7 conditional.3
  1165.1 2.9 fusion.8
  1169.2 6.7 conditional.3
  1173.1 2.9 fusion.8
  1177.2 6.7 conditional.3
  1181.1 2.9 fusion.8
  (310 shorter events, 156.7 us)
Async XLA Ops:
  7.2 8.1 copy-start
  7.2 168.8 %all-gather.9.cloned.1.call-start = ((), (), s32[]{:S(2)}) async-start(), calls=%async_computation.2 | async-start | bytes 4325376 | tf_op jit(solution)/shard_map/all_gather | solution.py:44
  11.7 535.8 %all-gather.5.cloned.1.call-start = ((), (), s32[]{:S(2)}) async-start(), calls=%async_computation | async-start | bytes 17301504 | tf_op jit(solution)/shard_map/all_gather | solution.py:78
  12.5 900.7 %all-gather.7.cloned.1.call-start = ((), (), s32[]{:S(2)}) async-start(), calls=%async_computation.1 | async-start | bytes 17301504 | tf_op jit(solution)/shard_map/all_gather | solution.py:79
  175.9 3.2 copy-start.2
  175.9 18.6 %copy-start.3 = (f32[512]{0:T(512)S(1)}, f32[512]{0:T(512)}, u32[]{:S(2)}) copy-start(f32[512]{0:T(512)} %param.17) | copy-start | bytes 6148
  1187.8 1.2 copy-start.1
Sparse Core Ops, SparseCore 0:
  11.8 164.0 all-gather.8
  177.7 369.7 all-gather.4
  549.3 363.8 all-gather.6
where the time goes:
time: 1220 us; the launch traced here: 1200 us
  waiting for transfers between devices  836 us (69%)
  matrix products  145 us (12%)
  local copies, waits for them, and re-layouts  100 us (8%)
  other arithmetic  62.8 us (5%)
  loops' own time  22.9 us (2%)
  blocking collectives  14.4 us (1%)
  between operations  13.9 us (1%)
    all_gather x1, waiting for transfers between devices, body(): key_piece = lax.all_gather(soft_key, 'ctx', axis=0, tiled=True)  351 us
    all_gather x1, waiting for transfers between devices, body(): value_piece = lax.all_gather(soft_value, 'ctx', axis=0, tiled=True)  327 us
    all_gather x1, waiting for transfers between devices, body(): lax.all_gather(local_state[None].astype(jnp.bfloat16), 'ctx', axis=0, til...  157 us
    dot_general x29, matrix products, compute(): jnp.einsum('hts,she->hte', probs, value_part, preferred_element_type=jnp....  82.8 us
    dot_general x29, matrix products, compute(): jnp.einsum('thd,shd->hts', soft_queries, key_part, preferred_element_type...  55.7 us
    unnamed x12, local copies, waits for them, and re-layouts  31.7 us
    reduce_sum x29, other arithmetic, compute(): new_total = total * shrink + jnp.sum(expo, axis=2)  30.2 us
  transfers between devices with their start and end apart: 3, of which 3 were waited for; matrix products, arithmetic and copies ran while one was open for 4% of the time, Pallas kernels for 0%

commit v1 on v0

v1 whole, which is shorter than its diff:
```python
import jax
import jax.numpy as jnp
from jax import lax
from jax.experimental import pallas as pl
from jax.experimental.pallas import tpu as pltpu
from jax.sharding import PartitionSpec as P

HEADS = 32
HD = 128
TOK = 512
MESH = pl.DeviceIdType.MESH
SCALE2 = HD**-0.5 * 1.4426950408889634
QT = 256
f32 = jnp.float32
bf16 = jnp.bfloat16


def dot_nt(a, b):
    return lax.dot_general(a, b, (((1,), (1,)), ((), ())), preferred_element_type=f32)


def dot_tn(a, b):
    return lax.dot_general(a, b, (((0,), (0,)), ((), ())), preferred_element_type=f32)


def kernel(
    lq, lk, lv, lg, gain, ld_ref, sq, sk, sv,
    lo, so,
    kv, qb, ob, m_ref, acc, mixed, st_send, st_recv, car_send, car_recv, ss_send, ss_recv,
    kv_sem, p1_sem, q_sem, q_send, fwd_sem, o_sem, o_send,
    st_ssem, st_rsem, car_ssem, car_rsem, ss_ssem, ss_rsem,
):
    c = lax.axis_index("ctx")
    h = lax.axis_index("head")
    y, x, zl = c // 8, (c // 2) % 4, c % 2
    zh, core = h // 2, h % 2
    slot = 2 * x + core

    def remote(src, dst, ssem, rsem, ctx, head):
        return pltpu.make_async_remote_copy(
            src_ref=src, dst_ref=dst, send_sem=ssem, recv_sem=rsem,
            device_id=(ctx, head), device_id_type=MESH,
        )

    def arrived(ref, sem):
        pltpu.make_async_copy(ref, ref, sem).wait()

    barrier = pltpu.get_barrier_semaphore()

    def hello(i, carry):
        pl.semaphore_signal(
            barrier, 1,
            device_id=((c + i // 2) % 32, zh * 2 + (core + i) % 2),
            device_id_type=MESH,
        )
        return carry

    lax.fori_loop(1, 64, hello, 0)

    def hello_head(i, carry):
        pl.semaphore_signal(barrier, 1, device_id=(c, (h + i) % 8), device_id_type=MESH)
        return carry

    lax.fori_loop(2 - core, 8 - core, hello_head, 0)
    pl.semaphore_wait(barrier, 69)

    odd = y % 2
    q_x = jnp.where(odd == 1, 3 - x, x)
    q_core = jnp.where(odd == 1, 1 - zl, zl)
    first = []
    for a in range(4):
        cols = pl.ds(a * HD, HD)
        for part, src in ((0, sk), (1, sv)):
            here = (a == y) & (core == zl)
            dst = kv.at[y, 2 * x + zl, part]
            sem = kv_sem.at[y, 2 * x + zl, part]
            first.append((here, remote(src.at[:, cols], dst, p1_sem.at[a, part], sem, a * 8 + x * 2 + core, zh * 2 + zl),
                          pltpu.make_async_copy(src.at[:, cols], dst, sem)))
    for a in range(4):
        cols = pl.ds(a * HD, HD)
        here = (a == y) & (core == zl) & (odd == 0)
        first.append((here, remote(sq.at[:, cols], qb.at[y], q_send.at[a], q_sem.at[y], a * 8 + q_x * 2 + core, zh * 2 + q_core),
                      pltpu.make_async_copy(sq.at[:, cols], qb.at[y], q_sem.at[y])))
    for here, far, near in first:
        @pl.when(here)
        def _():
            near.start()

        @pl.when(jnp.logical_not(here))
        def _():
            far.start()

    right = y * 8 + ((x + 1) % 4) * 2 + zl
    left = y * 8 + ((x + 3) % 4) * 2 + zl
    sib = zh * 2 + 1 - core

    def block(d):
        return 2 * ((x + d) % 4) + core

    def other(d):
        return 2 * ((x + d) % 4) + 1 - core

    def forward(s, b, ctx, head):
        remote(kv.at[s, b], kv.at[s, b], fwd_sem.at[s], kv_sem.at[s, b, 0], ctx, head).start()

    def own_piece(s):
        b = block(0)
        arrived(kv.at[s, b, 0], kv_sem.at[s, b, 0])
        arrived(kv.at[s, b, 1], kv_sem.at[s, b, 1])
        forward(s, b, right, h)
        forward(s, b, left, h)
        forward(s, b, c, sib)

    def from_sides(s):
        for d, part, ctx in ((3, 0, right), (1, 1, left)):
            b = block(d)
            arrived(kv.at[s, b], kv_sem.at[s, b, 0])
            remote(kv.at[s, b, part], kv.at[s, b, part], fwd_sem.at[s], kv_sem.at[s, b, part], ctx, h).start()
            forward(s, b, c, sib)

    def from_far(s):
        b = block(2)
        arrived(kv.at[s, b, 0], kv_sem.at[s, b, 0])
        arrived(kv.at[s, b, 1], kv_sem.at[s, b, 1])
        forward(s, b, c, sib)

    def from_sibling(s, d):
        b = other(d)
        arrived(kv.at[s, b], kv_sem.at[s, b, 0])

    def slice_at(k):
        return jnp.where(k == 0, y, jnp.where(k - 1 < y, k - 1, k))

    rows = lax.broadcasted_iota(jnp.int32, (TOK, HD), 0).astype(f32)

    def head_cols(a):
        return pl.ds(pl.multiple_of(a * HD, HD), HD)

    def states(a, carry):
        cols = head_cols(a)
        ld = ld_ref[a][:1, :]
        kd = (lk[:, cols].astype(f32) * jnp.exp((TOK - 1.0 - rows) * ld)).astype(bf16)
        st_send[head_cols(a), :] = dot_tn(kd, lv[:, cols]).astype(bf16)
        return carry

    lax.fori_loop(0, 4, states, 0)

    def scan_rows(i):
        return pl.ds(pl.multiple_of(i * 16, 16), 16)

    def send_state(i, carry):
        to = (c + i) % 32
        remote(st_send.at[scan_rows(to)], st_recv.at[scan_rows(c)], st_ssem, st_rsem, to, h).start()
        return carry

    lax.fori_loop(1, 32, send_state, 0)
    pltpu.make_async_copy(st_send.at[scan_rows(c)], st_recv.at[scan_rows(c)], st_rsem).start()

    own_piece(y)

    def intra(a, carry):
        cols = head_cols(a)
        ld = ld_ref[a][:1, :1]
        k = lk[:, cols]
        v = lv[:, cols]
        for i in range(2):
            n = (i + 1) * 256
            t = i * 256 + lax.broadcasted_iota(jnp.int32, (256, n), 0)
            s = lax.broadcasted_iota(jnp.int32, (256, n), 1)
            up = jnp.exp((i * 256 + lax.broadcasted_iota(jnp.int32, (256, 1), 0)).astype(f32) * ld)
            down = jnp.exp(-lax.broadcasted_iota(jnp.int32, (1, n), 1).astype(f32) * ld)
            w = dot_nt(lq[pl.ds(i * 256, 256), cols], k[:n]) * up * down
            w = jnp.where(t >= s, w, 0.0).astype(bf16)
            mixed[pl.ds(i * 256, 256), cols] = jnp.dot(w, v[:n], preferred_element_type=f32)
        return carry

    lax.fori_loop(0, 4, intra, 0)

    def scan_states():
        arrived(st_recv, st_rsem)
        f = jnp.exp(TOK * ld_ref[c // 8][:1, :])

        def step(b, carry):
            car_send[scan_rows(b), :] = carry.astype(bf16)
            return carry * f + st_recv[scan_rows(b), :].astype(f32)

        lax.fori_loop(0, 32, step, jnp.zeros((16, HD), f32))

        def send_carried(i, carry):
            to = (c + i) % 32
            remote(car_send.at[scan_rows(to)], car_recv.at[scan_rows(c)], car_ssem, car_rsem, to, h).start()
            return carry

        lax.fori_loop(1, 32, send_carried, 0)
        pltpu.make_async_copy(car_send.at[scan_rows(c)], car_recv.at[scan_rows(c)], car_rsem).start()

    def add_inter():
        arrived(car_recv, car_rsem)

        def one(a, squares):
            cols = head_cols(a)
            ld = ld_ref[a][:1, :]
            inter = jnp.dot(lq[:, cols], car_recv[head_cols(a), :], preferred_element_type=f32)
            both = mixed[:, cols] + jnp.exp((rows + 1.0) * ld) * inter
            mixed[:, cols] = both
            return squares + both * both

        squares = lax.fori_loop(0, 4, one, jnp.zeros((TOK, HD), f32))
        total = jnp.sum(squares.T, axis=0, keepdims=True)
        ss_send[...] = jnp.broadcast_to(total, (8, TOK))
        ss_recv[h] = ss_send[...]

        def send_squares(i, carry):
            remote(ss_send, ss_recv.at[h], ss_ssem, ss_rsem, c, (h + i) % 8).start()
            return carry

        lax.fori_loop(1, 8, send_squares, 0)

    def finish_light():
        arrived(ss_recv.at[pl.ds(0, 7)], ss_rsem)
        total = jnp.sum(ss_recv[...], axis=0)[:1, :]
        scale = lax.rsqrt(total / (HEADS * HD) + 1e-5)
        scale = jnp.broadcast_to(scale, (HD, TOK)).T
        for a in range(4):
            cols = pl.ds(a * HD, HD)
            gate = lg[:, cols].astype(f32)
            lo[:, cols] = (mixed[:, cols] * scale * gain[:, cols] / (1.0 + jnp.exp(-gate))).astype(bf16)

    m_ref[...] = jnp.full_like(m_ref, -1e30)
    acc[...] = jnp.zeros_like(acc)

    def tile(k, v, yq, q_at=None, k_at=None):
        n = k.shape[0]
        v2 = jnp.concatenate([v, jnp.ones_like(v)], axis=1)
        for i in range(TOK // QT):
            sl = pl.ds(i * QT, QT)
            s = dot_nt(qb[yq, sl, :], k)
            if q_at is not None:
                t = q_at + i * QT + lax.broadcasted_iota(jnp.int32, (QT, n), 0)
                j = k_at + lax.broadcasted_iota(jnp.int32, (QT, n), 1)
                s = jnp.where(t >= j, s, -1e30)
            old = m_ref[yq, sl, :]
            new = jnp.maximum(old, jnp.max(s, axis=1, keepdims=True))
            p = jnp.exp2((s - new[:, :1]) * SCALE2).astype(bf16)
            shrink = jnp.exp2((old - new) * SCALE2)
            acc[yq, sl, :] = acc[yq, sl, :] * jnp.concatenate([shrink, shrink], axis=1) + jnp.dot(
                p, v2, preferred_element_type=f32
            )
            m_ref[yq, sl, :] = new

    def pair(s, b):
        k = kv[s, pl.ds(2 * b, 2), 0].reshape(2 * TOK, HD)
        v = kv[s, pl.ds(2 * b, 2), 1].reshape(2 * TOK, HD)
        return k, v

    def full(s, d):
        def one(yq, carry):
            k, v = pair(s, (x + d) % 4)
            tile(k, v, yq)
            return carry

        lax.fori_loop(s + 1, 4, one, 0)

    def diagonal(s):
        r = jnp.where(s % 2 == 1, 7 - slot, slot)

        def one(b, carry):
            k, v = pair(s, b)
            tile(k, v, s)
            return carry

        lax.fori_loop(0, r // 2, one, 0)
        k, v = pair(s, r // 2)
        tile(k, v, s, r * TOK, (r // 2) * 2 * TOK)

    def o_copy(yq):
        ox = jnp.where(yq % 2 == 1, 3 - x, x)
        oz = jnp.where(yq % 2 == 1, 1 - core, core)
        here = (yq == y) & (core == zl) & (yq % 2 == 0)
        dst = so.at[:, head_cols(y)]
        far = remote(ob.at[yq], dst, o_send.at[yq], o_sem.at[y], yq * 8 + ox * 2 + oz, zh * 2 + zl)
        return here, far, pltpu.make_async_copy(ob.at[yq], dst, o_sem.at[y])

    def finish(yq):
        for i in range(TOK // QT):
            sl = pl.ds(i * QT, QT)
            ob[yq, sl, :] = (acc[yq, sl, :HD] / acc[yq, sl, HD:]).astype(bf16)
        here, far, near = o_copy(yq)

        @pl.when(here)
        def _():
            near.start()

        @pl.when(jnp.logical_not(here))
        def _():
            far.start()

    for i in range(4):
        arrived(qb.at[i], q_sem.at[i])

    def step(k, carry):
        s = slice_at(k)
        from_sibling(s, 0)
        full(s, 0)
        from_sides(s)

        @pl.when(k < 3)
        def _():
            own_piece(slice_at(k + 1))

        from_sibling(s, 3)
        full(s, 3)
        from_sibling(s, 1)
        full(s, 1)
        from_far(s)

        @pl.when(k == 0)
        def _():
            scan_states()

        @pl.when(k == 1)
        def _():
            add_inter()

        @pl.when(k == 2)
        def _():
            finish_light()

        from_sibling(s, 2)
        full(s, 2)
        diagonal(s)

        @pl.when((k >= 1) & (k <= y))
        def _():
            finish(k - 1)

        @pl.when(k >= y)
        def _():
            finish(k)

        return carry

    lax.fori_loop(0, 4, step, 0)

    for a in range(4):
        arrived(so.at[:, pl.ds(a * HD, HD)], o_sem.at[a])
        arrived(kv.at[a, pl.ds(0, 7)], fwd_sem.at[a])
        here, far, near = o_copy(a)

        @pl.when(jnp.logical_not(here))
        def _():
            far.wait_send()

    for here, far, near in first:
        @pl.when(jnp.logical_not(here))
        def _():
            far.wait_send()

    arrived(st_send.at[pl.ds(0, 31 * 16)], st_ssem)
    arrived(car_send.at[pl.ds(0, 31 * 16)], car_ssem)
    arrived(ss_recv.at[pl.ds(0, 7)], ss_ssem)


def body(lq, lk, lv, lg, gain, decay_exponent, sq, sk, sv):
    log_decay = -decay_exponent.astype(f32) / 65536.0
    ld = jnp.broadcast_to(log_decay[:, None, None], (4, 8, HD))
    vmem = pl.BlockSpec(memory_space=pltpu.VMEM)
    anywhere = pl.BlockSpec(memory_space=pl.ANY)
    dma = pltpu.SemaphoreType.DMA
    out = jax.ShapeDtypeStruct((TOK, 4 * HD), bf16)
    return pl.pallas_call(
        kernel,
        out_shape=(out, out),
        in_specs=[vmem] * 6 + [anywhere] * 3,
        out_specs=(vmem, anywhere),
        scratch_shapes=[
            pltpu.VMEM((4, 8, 2, TOK, HD), bf16),
            pltpu.VMEM((4, TOK, HD), bf16),
            pltpu.VMEM((4, TOK, HD), bf16),
            pltpu.VMEM((4, TOK, HD), f32),
            pltpu.VMEM((4, TOK, 2 * HD), f32),
            pltpu.VMEM((TOK, 4 * HD), f32),
            pltpu.VMEM((TOK, HD), bf16),
            pltpu.VMEM((TOK, HD), bf16),
            pltpu.VMEM((TOK, HD), bf16),
            pltpu.VMEM((TOK, HD), bf16),
            pltpu.VMEM((8, TOK), f32),
            pltpu.VMEM((8, 8, TOK), f32),
            dma((4, 8, 2)), dma((4, 2)), dma((4,)), dma((4,)), dma((4,)), dma((4,)), dma((4,)),
            dma, dma, dma, dma, dma, dma,
        ],
        compiler_params=pltpu.CompilerParams(
            collective_id=0, has_side_effects=True, vmem_limit_bytes=48 * 1024 * 1024
        ),
        name="layers",
    )(lq, lk, lv, lg, gain[None, :], ld, sq, sk, sv)


def solution(mesh):
    spec = P("ctx", "head")
    return jax.shard_map(
        body,
        mesh=mesh,
        in_specs=(spec, spec, spec, spec, P("head"), P("head"), spec, spec, spec),
        out_specs=(spec, spec),
        check_vma=False,
    )
```

time: 1220 us -> 122 us (0.10)
  the two profiles are of different devices: /device:TPU:28 before, /device:TPU:25 now
where the time goes in v1:
time: 122 us; the launch traced here: 121 us
  Pallas kernels  111 us (91%)
  local copies, waits for them, and re-layouts  10.2 us (8%)
    pallas_call x1, Pallas kernels, body(): pl.pallas_call(kernel, out_shape=(out, out), in_specs=[vmem] * 6 + [anywh...  111 us
    unnamed x20, local copies, waits for them, and re-layouts  10.1 us

profile of v1, /device:TPU:25, one launch (start us, length us, event | category | flops | bytes accessed | tf_op | source)
XLA Modules:
  0.0 121.5 jit_solution(13421151548941137515)
XLA Ops:
  0.6 0.0 copy-start.8
  0.6 0.6 copy-done.8
  1.3 0.0 copy-start.7
  1.3 0.1 broadcast_in_dim.10.ld_ref
  1.4 0.6 copy-done.7
  2.0 0.0 copy-start
  2.0 1.0 copy-done
  3.0 0.0 copy-start.1
  3.0 1.0 copy-done.1
  4.1 0.0 copy-start.2
  4.1 1.0 copy-done.2
  5.1 0.0 copy-start.3
  5.1 1.0 copy-done.3
  6.1 0.0 copy-start.4
  6.1 1.0 copy-done.4
  7.2 0.0 copy-start.5
  7.2 1.0 copy-done.5
  8.2 0.0 copy-start.6
  8.2 1.0 copy-done.6
  9.3 110.6 %layers.1 = (bf16[512,512]{1,0:T(8,128)(2,1)S(1)}, bf16[512,512]{1,0:T(8,128)(2,1)S(1)}) custom-call(bf16[512,512]{1,0:T(8,128)(2,1)S(1)} %copy-done, bf16[512,512]{1,0:T(8,128)(2,1)S(1)} %copy-done.1, bf16[512,512]{1,0:T(8,128)(2,1)S(1)} %copy-done.2, bf16[512,512]{1,0:T(8,128)(2,1)S(1)} %copy-done.3, f32[1,512]{1,0:T(1,128)S(1)} %bitcast.1, ...), custom_call_target="tpu_custom_call" | custom-call | tf_op jit(solution)/shard_map/layers/pallas_call | solution.py:371
  119.9 0.8 copy.13
  120.7 0.8 copy.14
  (1 shorter events, 0.0 us)
Async XLA Ops:
  0.6 0.7 copy-start.8
  1.3 0.7 copy-start.7
  2.0 1.0 copy-start
  3.0 1.0 copy-start.1
  4.1 1.0 copy-start.2
  5.1 1.0 copy-start.3
  6.1 1.0 copy-start.4
  7.2 1.0 copy-start.5
  8.2 1.0 copy-start.6

commit v2 on v1

v2 whole, which is shorter than its diff:
```python
import jax
import jax.numpy as jnp
from jax import lax
from jax.experimental import pallas as pl
from jax.experimental.pallas import tpu as pltpu
from jax.sharding import PartitionSpec as P

HEADS = 32
HD = 128
TOK = 512
MESH = pl.DeviceIdType.MESH
SCALE2 = HD**-0.5 * 1.4426950408889634
QT = 128
f32 = jnp.float32
bf16 = jnp.bfloat16


def dot_nt(a, b):
    return lax.dot_general(a, b, (((1,), (1,)), ((), ())), preferred_element_type=f32)


def dot_tn(a, b):
    return lax.dot_general(a, b, (((0,), (0,)), ((), ())), preferred_element_type=f32)


def kernel(
    lq_h, lk_h, lv_h, lg_h, gain, ld_ref, sq_h, sk_h, sv_h,
    lo, so,
    lq, lk, lv, lg, sq, sk, sv,
    kv, qb, ob, ol, m_ref, acc, mixed, home, home_l, o_in, l_in,
    st_send, st_recv, car_send, car_recv, ss_send, ss_recv,
    load_sem, kv_sem, p1_sem, q_sem, q_send, q_fwd, fwd_sem, o_sem, l_sem, o_send, l_send,
    st_ssem, st_rsem, car_ssem, car_rsem, ss_ssem, ss_rsem,
):
    c = lax.axis_index("ctx")
    h = lax.axis_index("head")
    y, x, zl = c // 8, (c // 2) % 4, c % 2
    zh, core = h // 2, h % 2
    sib = zh * 2 + 1 - core
    half = x // 2
    par = x % 2

    def remote(src, dst, ssem, rsem, ctx, head):
        return pltpu.make_async_remote_copy(
            src_ref=src, dst_ref=dst, send_sem=ssem, recv_sem=rsem,
            device_id=(ctx, head), device_id_type=MESH,
        )

    def arrived(ref, sem):
        pltpu.make_async_copy(ref, ref, sem).wait()

    def queries(n):
        return qb.at[n // 2, pl.ds(pl.multiple_of(n % 2 * TOK, TOK), TOK)]

    def head_cols(a):
        return pl.ds(pl.multiple_of(a * HD, HD), HD)

    barrier = pltpu.get_barrier_semaphore()

    def hello(i, carry):
        pl.semaphore_signal(
            barrier, 1,
            device_id=((c + i // 2) % 32, zh * 2 + (core + i) % 2),
            device_id_type=MESH,
        )
        return carry

    lax.fori_loop(1, 64, hello, 0)

    def hello_head(i, carry):
        pl.semaphore_signal(barrier, 1, device_id=(c, (h + i) % 8), device_id_type=MESH)
        return carry

    lax.fori_loop(2 - core, 8 - core, hello_head, 0)

    loads = [
        pltpu.make_async_copy(src, dst, load_sem.at[n])
        for n, (src, dst) in enumerate(
            ((lk_h, lk), (lv_h, lv), (lq_h, lq), (sq_h, sq), (sk_h, sk), (sv_h, sv), (lg_h, lg))
        )
    ]
    for load in loads:
        load.start()

    rows = lax.broadcasted_iota(jnp.int32, (TOK, HD), 0).astype(f32)
    loads[0].wait()
    loads[1].wait()

    for a in range(4):
        cols = pl.ds(a * HD, HD)
        ld = ld_ref[a][:1, :]
        kd = (lk[:, cols].astype(f32) * jnp.exp((TOK - 1.0 - rows) * ld)).astype(bf16)
        st_send[cols, :] = dot_tn(kd, lv[:, cols]).astype(bf16)

    m_ref[...] = jnp.full_like(m_ref, -1e30)
    acc[...] = jnp.zeros_like(acc)

    pl.semaphore_wait(barrier, 69)

    odd = y % 2
    q_x = jnp.where(odd == 1, 3 - x, x)
    q_core = jnp.where(odd == 1, 1 - zl, zl)
    q_at = 2 * y + q_x % 2

    def kv_copy(i, part):
        a = (y + i) % 4
        src = (sk_h, sv_h)[part].at[:, head_cols(a)]
        dst = kv.at[y, 2 * half + zl, part]
        sem = kv_sem.at[y, 2 * half + zl, part]
        zd = (core + a) % 2
        far = remote(src, dst, p1_sem.at[i, part], sem, a * 8 + x * 2 + zd, zh * 2 + zl)
        return (i == 0) & (zd == zl) & (core == zl), far, pltpu.make_async_copy(src, dst, sem)

    def q_copy(i):
        a = (y + i) % 4
        src = sq_h.at[:, head_cols(a)]
        dst, sem = queries(q_at), q_sem.at[q_at]
        zd = (core + a) % 2
        far = remote(src, dst, q_send.at[i], sem, a * 8 + q_x * 2 + zd, zh * 2 + q_core)
        return (i == 0) & (zd == zl) & (core == zl) & (odd == 0), far, pltpu.make_async_copy(src, dst, sem)

    def start(copy):
        here, far, near = copy

        @pl.when(here)
        def _():
            near.start()

        @pl.when(jnp.logical_not(here))
        def _():
            far.start()

    def wait_sent(copy):
        here, far, near = copy

        @pl.when(jnp.logical_not(here))
        def _():
            far.wait_send()

    start(kv_copy(0, 0))
    start(kv_copy(0, 1))
    for i in (0, 3, 2):
        start(q_copy(i))

    def scan_rows(i):
        return pl.ds(pl.multiple_of(i * 16, 16), 16)

    def send_state(i, carry):
        to = (c + i) % 32
        remote(st_send.at[scan_rows(to)], st_recv.at[scan_rows(c)], st_ssem, st_rsem, to, h).start()
        return carry

    lax.fori_loop(1, 32, send_state, 0)
    pltpu.make_async_copy(st_send.at[scan_rows(c)], st_recv.at[scan_rows(c)], st_rsem).start()

    loads[2].wait()

    def intra(heads):
        units = [(a, i) for a in heads for i in range(2)]

        def scores(a, i):
            cols = pl.ds(a * HD, HD)
            return dot_nt(lq[pl.ds(i * 256, 256), cols], lk[pl.ds(0, (i + 1) * 256), cols])

        s = scores(*units[0])
        for at, (a, i) in enumerate(units):
            ahead = scores(*units[at + 1]) if at + 1 < len(units) else None
            n = (i + 1) * 256
            cols = pl.ds(a * HD, HD)
            ld = ld_ref[a][:1, :1]
            t = i * 256 + lax.broadcasted_iota(jnp.int32, (256, n), 0)
            j = lax.broadcasted_iota(jnp.int32, (256, n), 1)
            up = jnp.exp((i * 256 + lax.broadcasted_iota(jnp.int32, (256, 1), 0)).astype(f32) * ld)
            down = jnp.exp(-lax.broadcasted_iota(jnp.int32, (1, n), 1).astype(f32) * ld)
            w = jnp.where(t >= j, s * up * down, 0.0).astype(bf16)
            mixed[pl.ds(i * 256, 256), cols] = jnp.dot(w, lv[pl.ds(0, n), cols], preferred_element_type=f32)
            s = ahead

    intra((0, 1, 2, 3))

    start(q_copy(1))
    start(kv_copy(3, 0))
    start(kv_copy(3, 1))

    def own_piece(s):
        b = 2 * half + core
        arrived(kv.at[s, b, 0], kv_sem.at[s, b, 0])
        arrived(kv.at[s, b, 1], kv_sem.at[s, b, 1])
        remote(kv.at[s, b], kv.at[s, b], fwd_sem.at[s], kv_sem.at[s, b, 0], y * 8 + (3 - x) * 2 + zl, h).start()
        remote(kv.at[s, b], kv.at[s, b], fwd_sem.at[s], kv_sem.at[s, b, 0], c, sib).start()

    def paired_piece(s):
        b = 2 * (1 - half) + core
        arrived(kv.at[s, b], kv_sem.at[s, b, 0])
        remote(kv.at[s, b], kv.at[s, b], fwd_sem.at[s], kv_sem.at[s, b, 0], c, sib).start()

    def slice_at(j):
        return (y + jnp.where(j == 2, 3, jnp.where(j == 3, 2, j))) % 4

    def place_of(s):
        d = (s - y + 4) % 4
        return jnp.where(d == 2, 3, jnp.where(d == 3, 2, d))

    own_piece(y)

    for n in (3, 4, 5):
        loads[n].wait()

    def at_home(heads):
        units = [(a, i) for a in heads for i in range(2)]

        def scores(a, i):
            cols = pl.ds(a * HD, HD)
            return dot_nt(sq[pl.ds(i * 256, 256), cols], sk[pl.ds(0, (i + 1) * 256), cols])

        s = scores(*units[0])
        for at, (a, i) in enumerate(units):
            ahead = scores(*units[at + 1]) if at + 1 < len(units) else None
            n = (i + 1) * 256
            sl = pl.ds(i * 256, 256)
            t = i * 256 + lax.broadcasted_iota(jnp.int32, (256, n), 0)
            j = lax.broadcasted_iota(jnp.int32, (256, n), 1)
            s = jnp.where(t >= j, s, -1e30)
            top = jnp.max(s, axis=1, keepdims=True)
            p = jnp.exp2((s - top) * SCALE2).astype(bf16)
            v = sv[pl.ds(0, n), pl.ds(a * HD, HD)]
            o = jnp.dot(p, jnp.concatenate([v, jnp.ones_like(v)], axis=1), preferred_element_type=f32)
            home[a, sl, :] = o[:, :HD] / o[:, HD:]
            home_l[a, sl, :] = top * SCALE2 + jnp.log2(o[:, HD:])
            s = ahead

    def pass_queries(i):
        yq = (y + i) % 4
        n = 2 * yq + par
        arrived(queries(n), q_sem.at[n])
        remote(queries(n), queries(n), q_fwd.at[i], q_sem.at[n], y * 8 + (x + 1 - 2 * par) * 2 + zl, h).start()

    at_home((0, 1))
    start(kv_copy(1, 0))
    start(kv_copy(1, 1))
    pass_queries(0)
    pass_queries(1)
    at_home((2, 3))
    start(kv_copy(2, 0))
    start(kv_copy(2, 1))
    pass_queries(2)
    pass_queries(3)

    def scan_states():
        arrived(st_recv, st_rsem)
        f = jnp.exp(TOK * ld_ref[c // 8][:1, :])

        def step(b, carry):
            car_send[scan_rows(b), :] = carry.astype(bf16)
            return carry * f + st_recv[scan_rows(b), :].astype(f32)

        lax.fori_loop(0, 32, step, jnp.zeros((16, HD), f32))

        def send_carried(i, carry):
            to = (c + i) % 32
            remote(car_send.at[scan_rows(to)], car_recv.at[scan_rows(c)], car_ssem, car_rsem, to, h).start()
            return carry

        lax.fori_loop(1, 32, send_carried, 0)
        pltpu.make_async_copy(car_send.at[scan_rows(c)], car_recv.at[scan_rows(c)], car_rsem).start()

    def add_inter():
        arrived(car_recv, car_rsem)

        def one(a, squares):
            cols = head_cols(a)
            ld = ld_ref[a][:1, :]
            inter = jnp.dot(lq[:, cols], car_recv[head_cols(a), :], preferred_element_type=f32)
            both = mixed[:, cols] + jnp.exp((rows + 1.0) * ld) * inter
            mixed[:, cols] = both
            return squares + both * both

        squares = lax.fori_loop(0, 4, one, jnp.zeros((TOK, HD), f32))
        total = jnp.sum(squares.T, axis=0, keepdims=True)
        ss_send[...] = jnp.broadcast_to(total, (8, TOK))
        ss_recv[h] = ss_send[...]

        def send_squares(i, carry):
            remote(ss_send, ss_recv.at[h], ss_ssem, ss_rsem, c, (h + i) % 8).start()
            return carry

        lax.fori_loop(1, 8, send_squares, 0)

    def finish_light():
        arrived(ss_recv.at[pl.ds(0, 7)], ss_rsem)
        loads[6].wait()
        total = jnp.sum(ss_recv[...], axis=0)[:1, :]
        scale = lax.rsqrt(total / (HEADS * HD) + 1e-5)
        scale = jnp.broadcast_to(scale, (HD, TOK)).T
        for a in range(4):
            cols = pl.ds(a * HD, HD)
            gate = lg[:, cols].astype(f32)
            lo[:, cols] = (mixed[:, cols] * scale * gain[:, cols] / (1.0 + jnp.exp(-gate))).astype(bf16)


    scan_states()
    own_piece(slice_at(1))

    def tile(k, v, yq, start_row, count):
        v2 = jnp.concatenate([v, jnp.ones_like(v)], axis=1)

        def piece(i):
            return pl.ds(start_row + i * QT, QT)

        def scores(i):
            return dot_nt(qb[yq, piece(i), :], k)

        def add(i, p, shrink):
            acc[yq, piece(i), :] = acc[yq, piece(i), :] * jnp.concatenate([shrink, shrink], axis=1) + jnp.dot(
                p, v2, preferred_element_type=f32
            )

        s = scores(0)
        behind = None
        for i in range(count // QT):
            ahead = scores(i + 1) if (i + 1) * QT < count else None
            old = m_ref[yq, piece(i), :]
            new = jnp.maximum(old, jnp.max(s, axis=1, keepdims=True))
            p = jnp.exp2((s - new[:, :1]) * SCALE2).astype(bf16)
            shrink = jnp.exp2((old - new) * SCALE2)
            m_ref[yq, piece(i), :] = new
            if behind is not None:
                add(*behind)
            behind = (i, p, shrink)
            s = ahead
        add(*behind)

    def query_home(n):
        yq, xd = n // 2, 2 * half + n % 2
        return jnp.where(yq % 2 == 1, 3 - xd, xd), jnp.where(yq % 2 == 1, 1 - core, core)

    def o_copies(n):
        yq = n // 2
        ox, oz = query_home(n)
        from_core = (zl + y) % 2
        here = (yq == y) & (ox == x) & (oz == zl) & (core == from_core)
        ctx, head = yq * 8 + ox * 2 + oz, zh * 2 + from_core
        return [
            (here, remote(src.at[n], dst.at[y, par], ssem.at[n], rsem.at[y, par], ctx, head),
             pltpu.make_async_copy(src.at[n], dst.at[y, par], rsem.at[y, par]))
            for src, dst, ssem, rsem in ((ob, o_in, o_send, o_sem), (ol, l_in, l_send, l_sem))
        ]

    def finish(n):
        yq, base = n // 2, pl.multiple_of(n % 2 * TOK, TOK)
        for i in range(2):
            sl, at = pl.ds(i * 256, 256), pl.ds(base + i * 256, 256)
            total = acc[yq, at, HD:]
            some = jnp.maximum(total, 1e-30)
            ob[n, sl, :] = (acc[yq, at, :HD] / some).astype(bf16)
            lse = jnp.where(total > 0.0, m_ref[yq, at, :] * SCALE2 + jnp.log2(some), -1e30)
            ol[n, :, sl] = lse.T[:8, :]
        for copy in o_copies(n):
            start(copy)

    paired_piece(y)

    def step(j, carry):
        s = slice_at(j)
        for part in range(2):
            b = 2 * part + 1 - core
            arrived(kv.at[s, b], kv_sem.at[s, b, 0])

        def one(i, carry):
            yq = (y + 1 + i) % 4

            @pl.when(j == 0)
            def _():
                n = 2 * yq + 1 - par
                arrived(queries(n), q_sem.at[n])

            @pl.when((i == 1) & (j < 2))
            def _():
                own_piece(slice_at(j + 2))

            @pl.when((i == 3) & (j < 3))
            def _():
                paired_piece(slice_at(j + 1))

            @pl.when((i == 2) & (j == 0))
            def _():
                add_inter()

            @pl.when((i == 2) & (j == 1))
            def _():
                finish_light()

            @pl.when(s < yq)
            def _():
                k = kv[s, :, 0].reshape(4 * TOK, HD)
                v = kv[s, :, 1].reshape(4 * TOK, HD)
                tile(k, v, yq, 0, 2 * TOK)

            @pl.when(s == yq)
            def _():
                def some(e, carry):
                    n, at = 2 * yq + e // 2, e % 2
                    xk = jnp.where(at == half, x, 3 - x)
                    row = pl.multiple_of(e // 2 * TOK, TOK)
                    ox, oz = query_home(n)

                    @pl.when(xk < ox)
                    def _():
                        k = kv[s, pl.ds(2 * at, 2), 0].reshape(2 * TOK, HD)
                        v = kv[s, pl.ds(2 * at, 2), 1].reshape(2 * TOK, HD)
                        tile(k, v, yq, row, TOK)

                    @pl.when((xk == ox) & (oz == 1))
                    def _():
                        tile(kv[s, 2 * at, 0], kv[s, 2 * at, 1], yq, row, TOK)

                    return carry

                lax.fori_loop(0, 4, some, 0)

            last = 0
            for e in range(4):
                last = jnp.maximum(last, jnp.where(e <= yq, place_of(e), 0))

            @pl.when(last == j)
            def _():
                finish(2 * yq)
                finish(2 * yq + 1)

            return carry

        return lax.fori_loop(0, 4, one, carry)

    lax.fori_loop(0, 4, step, 0)

    for i in (3, 2, 1, 0):
        a = (y + i) % 4
        cols = head_cols(a)
        for p in range(2):
            arrived(o_in.at[a, p], o_sem.at[a, p])
            arrived(l_in.at[a, p], l_sem.at[a, p])
        l0 = home_l[a]
        l1 = jnp.broadcast_to(l_in[a, 0][:1, :], (HD, TOK)).T
        l2 = jnp.broadcast_to(l_in[a, 1][:1, :], (HD, TOK)).T
        top = jnp.maximum(jnp.maximum(l0, l1), l2)
        w0, w1, w2 = jnp.exp2(l0 - top), jnp.exp2(l1 - top), jnp.exp2(l2 - top)
        o = w0 * home[a] + w1 * o_in[a, 0].astype(f32) + w2 * o_in[a, 1].astype(f32)
        so[:, cols] = (o / (w0 + w1 + w2)).astype(bf16)

    def end(n, carry):
        for copy in o_copies(n):
            wait_sent(copy)
        return carry

    lax.fori_loop(0, 8, end, 0)
    for i in range(4):
        arrived(kv.at[i, pl.ds(0, 3)], fwd_sem.at[i])
        arrived(qb.at[i, pl.ds(0, TOK)], q_fwd.at[i])
        wait_sent(kv_copy(i, 0))
        wait_sent(kv_copy(i, 1))
        wait_sent(q_copy(i))
    arrived(st_send.at[pl.ds(0, 31 * 16)], st_ssem)
    arrived(car_send.at[pl.ds(0, 31 * 16)], car_ssem)
    arrived(ss_recv.at[pl.ds(0, 7)], ss_ssem)


def body(lq, lk, lv, lg, gain, decay_exponent, sq, sk, sv):
    log_decay = -decay_exponent.astype(f32) / 65536.0
    ld = jnp.broadcast_to(log_decay[:, None, None], (4, 8, HD))
    vmem = pl.BlockSpec(memory_space=pltpu.VMEM)
    anywhere = pl.BlockSpec(memory_space=pl.ANY)
    dma = pltpu.SemaphoreType.DMA
    local = (TOK, 4 * HD)
    out = jax.ShapeDtypeStruct(local, bf16)
    return pl.pallas_call(
        kernel,
        out_shape=(out, out),
        in_specs=[anywhere] * 4 + [vmem] * 2 + [anywhere] * 3,
        out_specs=(vmem, vmem),
        scratch_shapes=[pltpu.VMEM(local, bf16)] * 7 + [
            pltpu.VMEM((4, 4, 2, TOK, HD), bf16),
            pltpu.VMEM((4, 2 * TOK, HD), bf16),
            pltpu.VMEM((8, TOK, HD), bf16),
            pltpu.VMEM((8, 8, TOK), f32),
            pltpu.VMEM((4, 2 * TOK, HD), f32),
            pltpu.VMEM((4, 2 * TOK, 2 * HD), f32),
            pltpu.VMEM(local, f32),
            pltpu.VMEM((4, TOK, HD), f32),
            pltpu.VMEM((4, TOK, HD), f32),
            pltpu.VMEM((4, 2, TOK, HD), bf16),
            pltpu.VMEM((4, 2, 8, TOK), f32),
            pltpu.VMEM((TOK, HD), bf16),
            pltpu.VMEM((TOK, HD), bf16),
            pltpu.VMEM((TOK, HD), bf16),
            pltpu.VMEM((TOK, HD), bf16),
            pltpu.VMEM((8, TOK), f32),
            pltpu.VMEM((8, 8, TOK), f32),
            dma((7,)), dma((4, 4, 2)), dma((4, 2)), dma((8,)), dma((4,)), dma((4,)), dma((4,)),
            dma((4, 2)), dma((4, 2)), dma((8,)), dma((8,)),
            dma, dma, dma, dma, dma, dma,
        ],
        compiler_params=pltpu.CompilerParams(
            collective_id=0, has_side_effects=True, vmem_limit_bytes=62 * 1024 * 1024
        ),
        name="layers",
    )(lq, lk, lv, lg, gain[None, :], ld, sq, sk, sv)


def solution(mesh):
    spec = P("ctx", "head")
    return jax.shard_map(
        body,
        mesh=mesh,
        in_specs=(spec, spec, spec, spec, P("head"), P("head"), spec, spec, spec),
        out_specs=(spec, spec),
        check_vma=False,
    )
```

time: 122 us -> 89.7 us (0.74)
  the two profiles are of different devices: /device:TPU:25 before, /device:TPU:56 now
where the time goes in v2:
time: 89.7 us; the launch traced here: 89.5 us
  Pallas kernels  84.8 us (95%)
  local copies, waits for them, and re-layouts  4.05 us (5%)
    pallas_call x1, Pallas kernels, body(): pl.pallas_call(kernel, out_shape=(out, out), in_specs=[anywhere] * 4 + [v...  84.8 us
    unnamed x6, local copies, waits for them, and re-layouts  3.37 us

profile of v2, /device:TPU:56, one launch (start us, length us, event | category | flops | bytes accessed | tf_op | source)
XLA Modules:
  0.0 89.5 jit_solution(11856160286189391067)
XLA Ops:
  0.6 0.0 copy-start.1
  0.6 0.6 copy-done.1
  1.3 0.7 broadcast_in_dim.10.ld_ref
  2.0 84.8 %layers.1 = (bf16[512,512]{1,0:T(8,128)(2,1)}, bf16[512,512]{1,0:T(8,128)(2,1)}) custom-call(bf16[512,512]{1,0:T(8,128)(2,1)} %lq_h.1, bf16[512,512]{1,0:T(8,128)(2,1)} %lk_h.1, bf16[512,512]{1,0:T(8,128)(2,1)} %lv_h.1, bf16[512,512]{1,0:T(8,128)(2,1)} %lg_h.1, f32[1,512]{1,0:T(1,128)} %bitcast.1, f32[4,8,128]{2,1,0:T(8,128)} %broadcast_in_dim.10.ld_ref, ...), custom_call_target="tpu_custom_call" | custom-call | tf_op jit(solution)/shard_map/layers/pallas_call | solution.py:475
  86.7 0.0 copy-start
  86.8 1.9 %copy.13 = bf16[512,512]{1,0:T(8,128)(2,1)} copy(bf16[512,512]{1,0:T(8,128)(2,1)} %get-tuple-element.4) | data formatting | bytes 1048576
  88.7 0.0 copy-done
  88.7 0.8 copy.14
  (1 shorter events, 0.0 us)
Async XLA Ops:
  0.6 0.7 copy-start.1
  86.7 1.9 %copy-start = (bf16[512,512]{1,0:T(8,128)(2,1)S(1)}, bf16[512,512]{1,0:T(8,128)(2,1)}, u32[]{:S(2)}) copy-start(bf16[512,512]{1,0:T(8,128)(2,1)} %get-tuple-element.5) | copy-start | bytes 1572868

commit v3 on v2

--- a/solution.py
+++ b/solution.py
@@ -97,10 +97,7 @@
 
     pl.semaphore_wait(barrier, 69)
 
-    odd = y % 2
-    q_x = jnp.where(odd == 1, 3 - x, x)
-    q_core = jnp.where(odd == 1, 1 - zl, zl)
-    q_at = 2 * y + q_x % 2
+    q_at = 2 * y + par
 
     def kv_copy(i, part):
         a = (y + i) % 4
@@ -116,8 +113,8 @@
         src = sq_h.at[:, head_cols(a)]
         dst, sem = queries(q_at), q_sem.at[q_at]
         zd = (core + a) % 2
-        far = remote(src, dst, q_send.at[i], sem, a * 8 + q_x * 2 + zd, zh * 2 + q_core)
-        return (i == 0) & (zd == zl) & (core == zl) & (odd == 0), far, pltpu.make_async_copy(src, dst, sem)
+        far = remote(src, dst, q_send.at[i], sem, a * 8 + x * 2 + zd, zh * 2 + zl)
+        return (i == 0) & (zd == zl) & (core == zl), far, pltpu.make_async_copy(src, dst, sem)
 
     def start(copy):
         here, far, near = copy
@@ -136,22 +133,22 @@
         @pl.when(jnp.logical_not(here))
         def _():
             far.wait_send()
+
+    def scan_rows(i):
+        return pl.ds(pl.multiple_of(i * 16, 16), 16)
+
+    def send_state(i, carry):
+        to = (c + i) % 32
+        remote(st_send.at[scan_rows(to)], st_recv.at[scan_rows(c)], st_ssem, st_rsem, to, h).start()
+        return carry
+
+    lax.fori_loop(1, 32, send_state, 0)
+    pltpu.make_async_copy(st_send.at[scan_rows(c)], st_recv.at[scan_rows(c)], st_rsem).start()
 
     start(kv_copy(0, 0))
     start(kv_copy(0, 1))
     for i in (0, 3, 2):
         start(q_copy(i))
-
-    def scan_rows(i):
-        return pl.ds(pl.multiple_of(i * 16, 16), 16)
-
-    def send_state(i, carry):
-        to = (c + i) % 32
-        remote(st_send.at[scan_rows(to)], st_recv.at[scan_rows(c)], st_ssem, st_rsem, to, h).start()
-        return carry
-
-    lax.fori_loop(1, 32, send_state, 0)
-    pltpu.make_async_copy(st_send.at[scan_rows(c)], st_recv.at[scan_rows(c)], st_rsem).start()
 
     loads[2].wait()
 
@@ -298,7 +295,6 @@
             lo[:, cols] = (mixed[:, cols] * scale * gain[:, cols] / (1.0 + jnp.exp(-gate))).astype(bf16)
 
 
-    scan_states()
     own_piece(slice_at(1))
 
     def tile(k, v, yq, start_row, count):
@@ -331,8 +327,7 @@
         add(*behind)
 
     def query_home(n):
-        yq, xd = n // 2, 2 * half + n % 2
-        return jnp.where(yq % 2 == 1, 3 - xd, xd), jnp.where(yq % 2 == 1, 1 - core, core)
+        return 2 * half + n % 2, core
 
     def o_copies(n):
         yq = n // 2
@@ -384,9 +379,13 @@
 
             @pl.when((i == 2) & (j == 0))
             def _():
+                scan_states()
+
+            @pl.when((i == 2) & (j == 1))
+            def _():
                 add_inter()
 
-            @pl.when((i == 2) & (j == 1))
+            @pl.when((i == 2) & (j == 3))
             def _():
                 finish_light()
 

time: 89.7 us -> 85.4 us (0.952)
  the two profiles are of different devices: /device:TPU:56 before, /device:TPU:28 now
where the time goes in v3:
time: 85.4 us; the launch traced here: 85.2 us
  Pallas kernels  80.5 us (94%)
  local copies, waits for them, and re-layouts  4.05 us (5%)
    pallas_call x1, Pallas kernels, body(): pl.pallas_call(kernel, out_shape=(out, out), in_specs=[anywhere] * 4 + [v...  80.5 us
    unnamed x6, local copies, waits for them, and re-layouts  3.37 us

profile of v3, /device:TPU:28, one launch (start us, length us, event | category | flops | bytes accessed | tf_op | source)
XLA Modules:
  0.0 85.2 jit_solution(6185830172509581969)
XLA Ops:
  0.6 0.0 copy-start.1
  0.6 0.6 copy-done.1
  1.3 0.7 broadcast_in_dim.10.ld_ref
  2.0 80.5 %layers.1 = (bf16[512,512]{1,0:T(8,128)(2,1)}, bf16[512,512]{1,0:T(8,128)(2,1)}) custom-call(bf16[512,512]{1,0:T(8,128)(2,1)} %lq_h.1, bf16[512,512]{1,0:T(8,128)(2,1)} %lk_h.1, bf16[512,512]{1,0:T(8,128)(2,1)} %lv_h.1, bf16[512,512]{1,0:T(8,128)(2,1)} %lg_h.1, f32[1,512]{1,0:T(1,128)} %bitcast.1, f32[4,8,128]{2,1,0:T(8,128)} %broadcast_in_dim.10.ld_ref, ...), custom_call_target="tpu_custom_call" | custom-call | tf_op jit(solution)/shard_map/layers/pallas_call | solution.py:474
  82.4 0.0 copy-start
  82.4 1.9 %copy.13 = bf16[512,512]{1,0:T(8,128)(2,1)} copy(bf16[512,512]{1,0:T(8,128)(2,1)} %get-tuple-element.4) | data formatting | bytes 1048576
  84.4 0.0 copy-done
  84.4 0.8 copy.14
  (1 shorter events, 0.0 us)
Async XLA Ops:
  0.6 0.7 copy-start.1
  82.4 1.9 %copy-start = (bf16[512,512]{1,0:T(8,128)(2,1)S(1)}, bf16[512,512]{1,0:T(8,128)(2,1)}, u32[]{:S(2)}) copy-start(bf16[512,512]{1,0:T(8,128)(2,1)} %get-tuple-element.5) | copy-start | bytes 1572868

commit v4 on v3

--- a/solution.py
+++ b/solution.py
@@ -24,7 +24,7 @@
 
 
 def kernel(
-    lq_h, lk_h, lv_h, lg_h, gain, ld_ref, sq_h, sk_h, sv_h,
+    lq_h, lk_h, lv_h, lg_h, gain, exponent, sq_h, sk_h, sv_h,
     lo, so,
     lq, lk, lv, lg, sq, sk, sv,
     kv, qb, ob, ol, m_ref, acc, mixed, home, home_l, o_in, l_in,
@@ -52,6 +52,9 @@
     def queries(n):
         return qb.at[n // 2, pl.ds(pl.multiple_of(n % 2 * TOK, TOK), TOK)]
 
+    def log_decay(a):
+        return jnp.full((1, HD), exponent[a], jnp.int32).astype(f32) * (-1.0 / 65536.0)
+
     def head_cols(a):
         return pl.ds(pl.multiple_of(a * HD, HD), HD)
 
@@ -88,7 +91,7 @@
 
     for a in range(4):
         cols = pl.ds(a * HD, HD)
-        ld = ld_ref[a][:1, :]
+        ld = log_decay(a)
         kd = (lk[:, cols].astype(f32) * jnp.exp((TOK - 1.0 - rows) * ld)).astype(bf16)
         st_send[cols, :] = dot_tn(kd, lv[:, cols]).astype(bf16)
 
@@ -164,7 +167,7 @@
             ahead = scores(*units[at + 1]) if at + 1 < len(units) else None
             n = (i + 1) * 256
             cols = pl.ds(a * HD, HD)
-            ld = ld_ref[a][:1, :1]
+            ld = log_decay(a)[:, :1]
             t = i * 256 + lax.broadcasted_iota(jnp.int32, (256, n), 0)
             j = lax.broadcasted_iota(jnp.int32, (256, n), 1)
             up = jnp.exp((i * 256 + lax.broadcasted_iota(jnp.int32, (256, 1), 0)).astype(f32) * ld)
@@ -245,7 +248,7 @@
 
     def scan_states():
         arrived(st_recv, st_rsem)
-        f = jnp.exp(TOK * ld_ref[c // 8][:1, :])
+        f = jnp.exp(TOK * log_decay(c // 8))
 
         def step(b, carry):
             car_send[scan_rows(b), :] = carry.astype(bf16)
@@ -266,7 +269,7 @@
 
         def one(a, squares):
             cols = head_cols(a)
-            ld = ld_ref[a][:1, :]
+            ld = log_decay(a)
             inter = jnp.dot(lq[:, cols], car_recv[head_cols(a), :], preferred_element_type=f32)
             both = mixed[:, cols] + jnp.exp((rows + 1.0) * ld) * inter
             mixed[:, cols] = both
@@ -464,17 +467,16 @@
 
 
 def body(lq, lk, lv, lg, gain, decay_exponent, sq, sk, sv):
-    log_decay = -decay_exponent.astype(f32) / 65536.0
-    ld = jnp.broadcast_to(log_decay[:, None, None], (4, 8, HD))
     vmem = pl.BlockSpec(memory_space=pltpu.VMEM)
     anywhere = pl.BlockSpec(memory_space=pl.ANY)
     dma = pltpu.SemaphoreType.DMA
     local = (TOK, 4 * HD)
+    smem = pl.BlockSpec(memory_space=pltpu.SMEM)
     out = jax.ShapeDtypeStruct(local, bf16)
     return pl.pallas_call(
         kernel,
         out_shape=(out, out),
-        in_specs=[anywhere] * 4 + [vmem] * 2 + [anywhere] * 3,
+        in_specs=[anywhere] * 4 + [vmem, smem] + [anywhere] * 3,
         out_specs=(vmem, vmem),
         scratch_shapes=[pltpu.VMEM(local, bf16)] * 7 + [
             pltpu.VMEM((4, 4, 2, TOK, HD), bf16),
@@ -502,7 +504,7 @@
             collective_id=0, has_side_effects=True, vmem_limit_bytes=62 * 1024 * 1024
         ),
         name="layers",
-    )(lq, lk, lv, lg, gain[None, :], ld, sq, sk, sv)
+    )(lq, lk, lv, lg, gain[None, :], decay_exponent, sq, sk, sv)
 
 
 def solution(mesh):

time: 85.4 us -> 84.6 us (level)
  local copies, waits for them, and re-layouts: 4.05 us -> 2.72 us
    unnamed x6 -> x4, local copies, waits for them, and re-layouts: 3.37 us -> 2.72 us
where the time goes in v4:
time: 84.6 us; the launch traced here: 84.5 us
  Pallas kernels  81.1 us (96%)
  local copies, waits for them, and re-layouts  2.72 us (3%)
    pallas_call x1, Pallas kernels, body(): pl.pallas_call(kernel, out_shape=(out, out), in_specs=[anywhere] * 4 + [v...  81.1 us
    unnamed x4, local copies, waits for them, and re-layouts  2.72 us

profile of v4, /device:TPU:28, one launch (start us, length us, event | category | flops | bytes accessed | tf_op | source)
XLA Modules:
  0.0 84.5 jit_solution(10595694989203217971)
XLA Ops:
  0.6 81.1 %layers.1 = (bf16[512,512]{1,0:T(8,128)(2,1)}, bf16[512,512]{1,0:T(8,128)(2,1)}) custom-call(bf16[512,512]{1,0:T(8,128)(2,1)} %lq_h.1, bf16[512,512]{1,0:T(8,128)(2,1)} %lk_h.1, bf16[512,512]{1,0:T(8,128)(2,1)} %lv_h.1, bf16[512,512]{1,0:T(8,128)(2,1)} %lg_h.1, f32[1,512]{1,0:T(1,128)} %bitcast.1, s32[4]{0:T(128)} %exponent.1, bf16[512,512]{1,0:T(8,128)(2,1)} %sq_h.1, ...), custom_call_target="tpu_custom_call" | custom-call | tf_op jit(solution)/shard_map/layers/pallas_call | solution.py:476
  81.7 0.0 copy-start
  81.8 1.9 %copy.13 = bf16[512,512]{1,0:T(8,128)(2,1)} copy(bf16[512,512]{1,0:T(8,128)(2,1)} %get-tuple-element.4) | data formatting | bytes 1048576
  83.7 0.0 copy-done
  83.7 0.8 copy.14
Async XLA Ops:
  81.7 1.9 %copy-start = (bf16[512,512]{1,0:T(8,128)(2,1)S(1)}, bf16[512,512]{1,0:T(8,128)(2,1)}, u32[]{:S(2)}) copy-start(bf16[512,512]{1,0:T(8,128)(2,1)} %get-tuple-element.5) | copy-start | bytes 1572868
